TPU v7x, 256 devices: a whole 4x4x8 slice. The times are simulated.
256 devices in a mesh: ctx: 32 (over z, x_hi, core), head: 8 (over x_lo, y).
Axes of the slice: x: 4 (x_hi: 2, x_lo: 2; x = x_hi * 2 + x_lo), y: 4, z: 8, core: 2. Of those that a mesh axis runs over, the one named last changes fastest.
Arguments:
- queries: bfloat16 [32768, 4096], P('ctx', 'head'), may hold values from -6 to 6
- token_keys: bfloat16 [32768, 4096], P('ctx', 'head'), may hold values from -6 to 6
- values: bfloat16 [32768, 4096], P('ctx', 'head'), may hold values from -6 to 6
- step_rates: float32 [8, 32768], P('head', 'ctx'), may hold values from 0.01 to 0.3
- window_blocks: int32 [8, 64], P('head', 'ctx'), may hold values from 0 to 2, as said below
- fast_gate: bfloat16 [8, 512, 512], P('head'), may hold values from -0.25 to 0.25
- fast_up: bfloat16 [8, 512, 512], P('head'), may hold values from -0.25 to 0.25
- fast_down: bfloat16 [8, 512, 512], P('head'), may hold values from -0.25 to 0.25
- norm_gain: float32 [8, 512], P('head'), may hold values from 0.1 to 1.9
- out_weight: bfloat16 [4096, 5120], P(None, 'head'), may hold values from -0.09375 to 0.09375
Outputs:
- layer_out: bfloat16 [32768, 5120], P('ctx', 'head')
Inputs may be any that keep to these rules, and one draw needn't show every extreme that they name: `window_blocks`: how many earlier blocks of 512 tokens each query block of each head may see.
All inputs are finite; a program needn't handle non-finite values.
Results may differ from a plain program's by a relative error of at most 0.029.
Values may be sent and summed in bfloat16 or wider, within the bound.
A program may use at most 64 MiB of HBM per device.

v0:
```python
import jax
import jax.numpy as jnp
from jax import lax
from jax.sharding import PartitionSpec as P

HD = 512
BL = 512
WIN = 2


grad_limit = 24.0
epsilon = 1e-06


def from_behind(block, axis, distance):
    devices = range(lax.axis_size(axis))
    route = [(i - distance, i) for i in devices if i - distance in devices]
    return lax.ppermute(block, axis, route)


def silu_pair(inputs):
    sigmoid = jax.nn.sigmoid(inputs)
    return (inputs * sigmoid, sigmoid * (1.0 + inputs * (1.0 - sigmoid)))


def renewed(weight, gradient, factor):
    start_weight = weight.astype(jnp.float32)
    moved = start_weight - factor * gradient
    before = jnp.sqrt(jnp.sum(start_weight * start_weight, axis=-2, keepdims=True) + epsilon)
    after = jnp.sqrt(jnp.sum(moved * moved, axis=-2, keepdims=True) + epsilon)
    return (moved * (before / after)).astype(jnp.bfloat16)


def head_squares(grad_gate, grad_up, grad_down):
    return (
        jnp.sum(grad_gate * grad_gate, axis=(1, 2))
        + jnp.sum(grad_up * grad_up, axis=(1, 2))
        + jnp.sum(grad_down * grad_down, axis=(1, 2))
    )


def per_device(
    queries,
    token_keys,
    values,
    step_rates,
    window_blocks,
    fast_gate,
    fast_up,
    fast_down,
    norm_gain,
    out_weight,
):
    tok_rows = queries.shape[0]
    head_count = fast_gate.shape[0]
    head_width = fast_gate.shape[1]
    halo_rows = WIN * BL
    prev_keys, prev_values = from_behind((token_keys, values), "ctx", 1)
    query_heads = queries.reshape(tok_rows, head_count, head_width)
    key_heads = token_keys.reshape(tok_rows, head_count, head_width)
    value_heads = values.reshape(tok_rows, head_count, head_width)
    gate_pre = jnp.einsum("thd,hdf->thf", key_heads, fast_gate, preferred_element_type=jnp.float32)
    up_pre = jnp.einsum("thd,hdf->thf", key_heads, fast_up, preferred_element_type=jnp.float32)
    silu_val, silu_slope = silu_pair(gate_pre)
    hidden_act = (silu_val * up_pre).astype(jnp.bfloat16)
    target = (-step_rates.T[:, :, None] * value_heads.astype(jnp.float32)).astype(jnp.bfloat16)
    grad_down = jnp.einsum("thf,thd->hfd", hidden_act, target, preferred_element_type=jnp.float32)
    back_act = jnp.einsum("thd,hfd->thf", target, fast_down, preferred_element_type=jnp.float32)
    back_gate = (back_act * up_pre * silu_slope).astype(jnp.bfloat16)
    back_up = (back_act * silu_val).astype(jnp.bfloat16)
    grad_gate = jnp.einsum("thd,thf->hdf", key_heads, back_gate, preferred_element_type=jnp.float32)
    grad_up = jnp.einsum("thd,thf->hdf", key_heads, back_up, preferred_element_type=jnp.float32)
    grad_gate, grad_up, grad_down = (
        lax.psum(grad_gate.astype(jnp.bfloat16), "ctx").astype(jnp.float32),
        lax.psum(grad_up.astype(jnp.bfloat16), "ctx").astype(jnp.float32),
        lax.psum(grad_down.astype(jnp.bfloat16), "ctx").astype(jnp.float32),
    )
    gnorm = jnp.sqrt(head_squares(grad_gate, grad_up, grad_down) + epsilon)
    factor = jnp.minimum(1.0, grad_limit / gnorm)[:, None, None]
    new_gate = renewed(fast_gate, grad_gate, factor)
    new_up = renewed(fast_up, grad_up, factor)
    new_down = renewed(fast_down, grad_down, factor)
    query_gate = jnp.einsum(
        "thd,hdf->thf", query_heads, new_gate, preferred_element_type=jnp.float32
    )
    query_up = jnp.einsum("thd,hdf->thf", query_heads, new_up, preferred_element_type=jnp.float32)
    query_silu, unused_slope = silu_pair(query_gate)
    read_act = (query_silu * query_up).astype(jnp.bfloat16)
    fast_out = jnp.einsum("thf,hfd->thd", read_act, new_down, preferred_element_type=jnp.float32)
    normed = (
        fast_out
        * lax.rsqrt(jnp.mean(fast_out * fast_out, axis=-1, keepdims=True) + epsilon)
        * norm_gain[None, :, :]
    )
    extended_keys = jnp.concatenate([prev_keys, token_keys], axis=0).reshape(
        halo_rows + tok_rows, head_count, head_width
    )
    extended_values = jnp.concatenate([prev_values, values], axis=0).reshape(
        halo_rows + tok_rows, head_count, head_width
    )
    local_blocks = tok_rows // BL
    first_block = lax.axis_index("ctx") * local_blocks
    score_scale = HD ** (-0.5)

    def one_block(block_id):
        global_block = first_block + block_id
        query_block = lax.dynamic_slice_in_dim(query_heads, block_id * BL, BL, 0)
        key_block = lax.dynamic_slice_in_dim(extended_keys, block_id * BL, (WIN + 1) * BL, 0)
        value_block = lax.dynamic_slice_in_dim(extended_values, block_id * BL, (WIN + 1) * BL, 0)
        scores = (
            jnp.einsum("qhd,khd->hqk", query_block, key_block, preferred_element_type=jnp.float32)
            * score_scale
        )
        query_pos = global_block * BL + jnp.arange(BL, dtype=jnp.int32)
        key_pos = global_block * BL - halo_rows + jnp.arange((WIN + 1) * BL, dtype=jnp.int32)
        reach_blocks = lax.dynamic_index_in_dim(window_blocks, block_id, 1, keepdims=False)
        visible = (
            (key_pos[None, None, :] <= query_pos[None, :, None])
            & (key_pos[None, None, :] >= 0)
            & (key_pos[None, None, :] // BL >= global_block - reach_blocks[:, None, None])
        )
        scores = jnp.where(visible, scores, -jnp.inf)
        row_top = jnp.max(scores, axis=-1, keepdims=True)
        raised = jnp.exp(scores - row_top)
        weights_bf = (raised / jnp.sum(raised, axis=-1, keepdims=True)).astype(jnp.bfloat16)
        return jnp.einsum(
            "hqk,khd->qhd", weights_bf, value_block, preferred_element_type=jnp.float32
        )

    attended = lax.map(one_block, jnp.arange(local_blocks, dtype=jnp.int32)).reshape(
        tok_rows, head_count, head_width
    )
    readout = (normed + attended).astype(jnp.bfloat16).reshape(tok_rows, head_count * head_width)
    layer_out = jnp.dot(
        lax.all_gather(readout, "head", axis=1, tiled=True),
        out_weight,
        preferred_element_type=jnp.float32,
    )
    return layer_out.astype(jnp.bfloat16)


def solution(mesh):
    placed = (
        P("ctx", "head"),
        P("ctx", "head"),
        P("ctx", "head"),
        P("head", "ctx"),
        P("head", "ctx"),
        P("head", None, None),
        P("head", None, None),
        P("head", None, None),
        P("head", None),
        P(None, "head"),
    )
    return jax.shard_map(
        per_device, mesh=mesh, in_specs=placed, out_specs=P("ctx", "head"), check_vma=False
    )
```

profile of v0, /device:TPU:2, one launch (start us, length us, event | category | flops | bytes accessed | tf_op | source)
XLA Modules:
  0.0 430.1 jit_solution(16107011768938937581)
XLA Ops:
  6.5 2.9 collective-permute-start
  9.4 4.3 %collective-permute-start.1 = (bf16[1024,512]{1,0:T(8,128)(2,1)}, bf16[1024,512]{1,0:T(8,128)(2,1)}, u32[]{:S(2)}, u32[]{:S(2)}) collective-permute-start(bf16[1024,512]{1,0:T(8,128)(2,1)} %param.13), channel_id=1, source_target_pairs={{0,8},{8,16},{16,24},{24,32},{32,40},{40,48},{48,56},{56,64},{64,7... | collective-permute-start | bytes 3145736 | tf_op jit(solution)/shard_map/ppermute | solution.py:18
  13.7 2.1 fusion.68
  17.9 2.0 fusion.44
  21.5 2.1 fusion.42
  24.1 2.1 copy.20
  26.2 2.1 copy.26
  28.3 2.7 maximum_bitcast_fusion
  31.1 2.7 maximum_bitcast_fusion.1
  33.8 62.4 %while.12 = (s32[]{:T(128)}, f32[2,512,1,512]{1,0,3,2:T(2,128)}, s32[2]{0:T(128)S(1)}, bf16[2048,1,512]{2,0,1:T(8,128)(2,1)}, s32[]{:T(128)}, /*index=5*/s32[1,2...) while((s32[]{:T(128)}, f32[2,512,1,512]{1,0,3,2:T(2,128)}, ...), condition=%wide.region_16.17_spmd, body=%wide.region_13.16_spmd.sunk | while | flops 1619292160 | bytes 26774912 | solution.py:130
  38.9 2.7 fusion.100
  45.6 19.4 %dynamic_update_slice.8 = f32[2,512,1,512]{1,0,3,2:T(2,128)} dynamic-update-slice(f32[2,512,1,512]{1,0,3,2:T(2,128)} %get-tuple-element.215, f32[1,512,1,512]{1,0,3,2:T(1,128)S(1)} %copy.47, s32[]{:T(128)S(6)} %copy.51, s32[]{:T(128)} %constant.105.clone.1..sunk, s32[]{:T(128)} %constant.105.clone.1..sunk, s32[]{:T(128)} %constant.105.clone.1..sunk) | dynamic-update-slice | bytes 2097156 | tf_op jit(solution)/shard_map/while/body/jit(dynamic_update_index_in_dim)/dynamic_update_slice | solution.py:130
  70.1 2.7 fusion.100
  76.8 19.4 %dynamic_update_slice.8 = f32[2,512,1,512]{1,0,3,2:T(2,128)} dynamic-update-slice(f32[2,512,1,512]{1,0,3,2:T(2,128)} %get-tuple-element.215, f32[1,512,1,512]{1,0,3,2:T(1,128)S(1)} %copy.47, s32[]{:T(128)S(6)} %copy.51, s32[]{:T(128)} %constant.105.clone.1..sunk, s32[]{:T(128)} %constant.105.clone.1..sunk, s32[]{:T(128)} %constant.105.clone.1..sunk) | dynamic-update-slice | bytes 2097156 | tf_op jit(solution)/shard_map/while/body/jit(dynamic_update_index_in_dim)/dynamic_update_slice | solution.py:130
  96.2 3.1 reshape.305
  99.3 197.9 %all-reduce.3.cloned.1.call-done = (bf16[1,512,512]{1,2,0:T(8,128)(2,1)}, bf16[1,512,512]{1,2,0:T(8,128)(2,1)}, bf16[1,512,512]{1,2,0:T(8,128)(2,1)}) async-done(((bf16[1,512,512]{1,2,0:T(8,128)(2,1)}, bf16[1,512,512]{1,2,0:T(8,128)(2,1)}, bf16[1,512,512]{1,2,0:T(8,128)(2,1)}), (bf16[1,512,512]{1,2,0:T(8,128)(2,1)}, bf16[1,512,512]{1,2,0:T(8,128)(2,1)}, ...) | async-done | bytes 1572880 | tf_op jit(solution)/shard_map/psum | solution.py:74
  297.2 2.0 fusion.46
  299.2 2.0 fusion.47
  305.0 2.1 fusion.45
  307.2 2.2 fusion.61
  309.8 5.6 %fusion.23 = (f32[1024]{0:T(1024)S(1)}, f32[512,1024]{1,0:T(8,128)}) fusion(bf16[1024,512]{1,0:T(8,128)(2,1)} %param.12, f32[512,1024]{0,1:T(8,128)} %fusion.61, bf16[1,512,512]{1,2,0:T(8,128)(2,1)} %get-tuple-element.132, bf16[1,512,512]{1,2,0:T(8,128)(2,1)} %copy.26, f32[]{:T(128)S(6)} %min.4, f32[512]{0:T(512)S(1)} %rsqrt_multiply_fusion, ...), kind=kOutput, calls=%fused_computation.38 | convolution fusion | flops 1081080832 | bytes 7348228 | tf_op jit(solution)/shard_map/thf,hfd->thd/dot_general | solution.py:89
  315.4 2.9 fusion.22
  318.2 93.5 %all-gather.3.cloned.1.call-done = bf16[1024,1,4096]{0,2,1:T(8,128)(2,1)} async-done(((bf16[1024,1,512]{0,2,1:T(8,128)(2,1)}), bf16[1024,1,4096]{0,2,1:T(8,128)(2,1)}) %all-gather.3.cloned.1.call-update) | async-done | bytes 8388624 | tf_op jit(solution)/shard_map/all_gather | solution.py:135
  411.7 11.5 %fusion.37 = bf16[1024,640]{1,0:T(8,128)(2,1)} fusion(bf16[4096,640]{1,0:T(8,128)(2,1)} %param.21, bf16[1024,1,4096]{0,2,1:T(8,128)(2,1)} %all-gather.3.cloned.1.call-done), kind=kOutput, calls=%fused_computation.61 | convolution fusion | flops 5369364480 | bytes 14942208 | tf_op jit(solution)/shard_map/dot_general | solution.py:134
  (63 shorter events, 16.8 us)
Async XLA Ops:
  6.5 9.3 %copy-start = (bf16[1024,512]{1,0:T(8,128)(2,1)S(1)}, bf16[1024,512]{1,0:T(8,128)(2,1)}, u32[]{:S(2)}) copy-start(bf16[1024,512]{1,0:T(8,128)(2,1)} %param.13) | copy-start | bytes 3145732
  6.5 9.3 %copy-start.10 = (f32[1,1024]{1,0:T(1,128)S(1)}, f32[1,1024]{1,0:T(1,128)}, u32[]{:S(2)}) copy-start(f32[1,1024]{1,0:T(1,128)} %param.15) | copy-start | bytes 12292
  6.5 9.3 %copy-start.3 = (bf16[1,512,512]{2,1,0:T(8,128)(2,1)S(1)}, bf16[1,512,512]{2,1,0:T(8,128)(2,1)}, u32[]{:S(2)}) copy-start(bf16[1,512,512]{2,1,0:T(8,128)(2,1)} %param.17) | copy-start | bytes 1572868
  6.5 290.6 %all-reduce.3.cloned.1.call-start = ((), (), s32[]{:S(2)}) async-start(), calls=%async_computation.1 | async-start | bytes 3145728 | tf_op jit(solution)/shard_map/psum | solution.py:74
  6.5 21.8 %collective-permute-start = (bf16[1024,512]{1,0:T(8,128)(2,1)}, bf16[1024,512]{1,0:T(8,128)(2,1)}, u32[]{:S(2)}, u32[]{:S(2)}) collective-permute-start(bf16[1024,512]{1,0:T(8,128)(2,1)} %param.14), channel_id=1, source_target_pairs={{0,8},{8,16},{16,24},{24,32},{32,40},{40,48},{48,56},{56,64},{64,7... | collective-permute-start | bytes 3145736 | tf_op jit(solution)/shard_map/ppermute | solution.py:18
  9.4 21.6 %collective-permute-start.1 = (bf16[1024,512]{1,0:T(8,128)(2,1)}, bf16[1024,512]{1,0:T(8,128)(2,1)}, u32[]{:S(2)}, u32[]{:S(2)}) collective-permute-start(bf16[1024,512]{1,0:T(8,128)(2,1)} %param.13), channel_id=1, source_target_pairs={{0,8},{8,16},{16,24},{24,32},{32,40},{40,48},{48,56},{56,64},{64,7... | collective-permute-start | bytes 3145736 | tf_op jit(solution)/shard_map/ppermute | solution.py:18
  15.8 1.2 copy-start.2
  15.8 1.3 copy-start.7
  23.6 388.1 %all-gather.3.cloned.1.call-start = ((), (), s32[]{:S(2)}) async-start(), calls=%async_computation | async-start | bytes 9437184 | tf_op jit(solution)/shard_map/all_gather | solution.py:135
  31.0 2.8 copy-start.8
  31.0 2.8 copy-start.12
  41.7 1.6 copy-start.4
  72.9 1.6 copy-start.4
  297.2 9.9 %copy-start.1 = (bf16[1,512,512]{1,2,0:T(8,128)(2,1)S(1)}, bf16[1,512,512]{1,2,0:T(8,128)(2,1)}, u32[]{:S(2)}) copy-start(bf16[1,512,512]{1,2,0:T(8,128)(2,1)} %get-tuple-element.131) | copy-start | bytes 1572868
  305.0 2.1 copy-start.9
  307.1 2.3 copy-start.5
  307.2 2.2 copy-start.6
  309.8 5.6 %copy-start.11 = (f32[1,512]{1,0:T(1,128)S(1)}, f32[1,512]{1,0:T(1,128)}, u32[]{:S(2)}) copy-start(f32[1,512]{1,0:T(1,128)} %param.20) | copy-start | bytes 6148
Sparse Core Ops, SparseCore 0:
  23.8 273.3 all-reduce.2
  318.4 93.3 all-gather.2
where the time goes:
time: 435 us; the launch traced here: 430 us
  waiting for transfers between devices  291 us (67%)
  local copies, waits for them, and re-layouts  53.7 us (12%)
  matrix products  36.4 us (8%)
  other arithmetic  17.9 us (4%)
  between operations  15.5 us (4%)
  loops' own time  7.75 us (2%)
  starting transfers between devices  7.43 us (2%)
    psum x1, waiting for transfers between devices, per_device(): lax.psum(grad_gate.astype(jnp.bfloat16), 'ctx').astype(jnp.float32)  198 us
    all_gather x1, waiting for transfers between devices, per_device(): lax.all_gather(readout, 'head', axis=1, tiled=True)  93.5 us
    dynamic_update_slice x4, local copies, waits for them, and re-layouts, per_device(): lax.map(one_block, jnp.arange(local_blocks, dtype=jnp.int32))  41 us
    dot_general x1, matrix products, per_device(): jnp.dot(lax.all_gather(readout, 'head', axis=1, tiled=True), out_weight,...  11.5 us
  transfers between devices with their start and end apart: 4, of which 2 were waited for; matrix products, arithmetic and copies ran while one was open for 17% of the time, Pallas kernels for 0%

commit v1 on v0

v1 whole, which is shorter than its diff:
```python
import jax
import jax.numpy as jnp
from jax import lax
from jax.sharding import PartitionSpec as P
from jax.experimental import pallas as pl
from jax.experimental.pallas import tpu as pltpu

MESH = pl.DeviceIdType.MESH
F32 = jnp.float32
BF16 = jnp.bfloat16

TOK = 1024
HD = 512
BL = 512
HALO = 1024
NZ = 8
NY = 4
HEADS = 8
COLS = 640
HALF = 256
QUART = 128
SHARD = 16
TT = 256
NT = TOK // TT
GT = 128
NG = TOK // GT
GRAD_LIMIT = 24.0
EPS = 1e-6
MASKED = -1e30


def sigmoid(x):
    return 0.5 * jnp.tanh(0.5 * x) + 0.5


def dot(a, b):
    return jnp.dot(a, b, preferred_element_type=F32)


def dot_nt(a, b):
    return lax.dot_general(a, b, (((1,), (1,)), ((), ())), preferred_element_type=F32)


def dot_tn(a, b):
    return lax.dot_general(a, b, (((0,), (0,)), ((), ())), preferred_element_type=F32)


def tile_kind(t):
    return "A" if t % 2 == 0 else "B"


def body(
    q_ref, k_ref, v_ref, rate_ref, win_ref, w1_ref, w3_ref, w2_ref, gain_ref, wo_ref,
    out_ref,
    q, k, v, hk, hv, w1, w3, w2, wo, rate, gain,
    hid, tgt, bg, bu,
    sib_send, sib_recv, own, xh_send, xh_recv, z_send, z_recv, gfull,
    n1, n3, n2, m_run, l_run, acc, gat, outv,
    load_sem, out_sem, halo_ss, halo_rs, sib_ss, sib_rs, xh_ss, xh_rs, z_ss, z_rs,
    ag_ss, ag_rs, xg_ss, xg_rs, sg_ss, sg_rs, gy_ss, gx_ss, g_rs,
):
    ctx = lax.axis_index("ctx")
    head = lax.axis_index("head")
    z = ctx // 4
    xh = (ctx // 2) % 2
    core = ctx % 2
    xl = head // 4
    y = head % 4

    def at_ctx(zz, xx, cc):
        return (zz * 4 + xx * 2 + cc, head)

    def at_head(xx, yy):
        return (ctx, xx * 4 + yy)

    sib = at_ctx(z, xh, 1 - core)
    xhp = at_ctx(z, 1 - xh, core)
    zpeer = [None] + [at_ctx((z + d) % NZ, xh, core) for d in range(1, NZ)]
    nxt = ((ctx + 1) % 32, head)
    prv = ((ctx + 31) % 32, head)
    xp = at_head(1 - xl, y)
    yp = at_head(xl, (y + 1) % NY)
    ym = at_head(xl, (y + 3) % NY)

    bar = pltpu.get_barrier_semaphore()
    partners = [sib, xhp] + zpeer[1:] + [xp, yp, ym, prv]
    for p in partners:
        pl.semaphore_signal(bar, inc=1, device_id=p, device_id_type=MESH)

    loads = []
    for i, (src, dst) in enumerate(
        ((k_ref, k), (w1_ref, w1), (w3_ref, w3), (w2_ref, w2), (rate_ref, rate), (v_ref, v),
         (q_ref, q), (gain_ref, gain), (wo_ref, wo))
    ):
        c = pltpu.make_async_copy(src, dst, load_sem.at[i])
        c.start()
        loads.append(c)

    pl.semaphore_wait(bar, len(partners))

    sends = []

    def send(src, dst, ss, rs, dev):
        c = pltpu.make_async_remote_copy(
            src_ref=src, dst_ref=dst, send_sem=ss, recv_sem=rs, device_id=dev, device_id_type=MESH
        )
        c.start()
        sends.append(c)
        return c

    def arrived(dst, rs):
        pltpu.make_async_remote_copy(
            src_ref=dst, dst_ref=dst, send_sem=rs, recv_sem=rs, device_id=sib, device_id_type=MESH
        ).wait_recv()

    send(k_ref, hk, halo_ss.at[0], halo_rs.at[0], nxt)
    send(v_ref, hv, halo_ss.at[1], halo_rs.at[1], nxt)

    for c in loads[:6]:
        c.wait()

    def grad_tile(t, carry):
        r = pl.ds(pl.multiple_of(t * TT, TT), TT)
        kt = k[r, :]
        gp = dot(kt, w1[0])
        up = dot(kt, w3[0])
        s = sigmoid(gp)
        sv = gp * s
        hid[r, :] = (sv * up).astype(BF16)
        row = rate[:, r]
        eye = lax.broadcasted_iota(jnp.int32, (TT, TT), 0) == lax.broadcasted_iota(
            jnp.int32, (TT, TT), 1
        )
        col = jnp.sum(jnp.where(eye, row, 0.0), axis=1, keepdims=True)
        tg = (-col * v[r, :].astype(F32)).astype(BF16)
        tgt[r, :] = tg
        ba = dot_nt(tg, w2[0])
        bg[r, :] = (ba * up * (s * (1.0 + gp * (1.0 - s)))).astype(BF16)
        bu[r, :] = (ba * sv).astype(BF16)
        return carry

    lax.fori_loop(0, NT, grad_tile, 0)

    theirs = pl.ds(pl.multiple_of((1 - core) * HALF, HALF), HALF)
    mine = pl.ds(pl.multiple_of(core * HALF, HALF), HALF)
    pairs = ((hid, tgt), (k, bg), (k, bu))
    for m, (a, b) in enumerate(pairs):
        sib_send[m] = dot_tn(a[:, theirs], b[...]).astype(BF16)
        send(sib_send.at[m], sib_recv.at[m], sib_ss.at[m], sib_rs.at[m], sib)
    for m, (a, b) in enumerate(pairs):
        own[m] = dot_tn(a[:, mine], b[...])

    x_theirs = pl.ds(pl.multiple_of((1 - xh) * QUART, QUART), QUART)
    x_mine = pl.ds(pl.multiple_of(xh * QUART, QUART), QUART)
    for m in range(3):
        arrived(sib_recv.at[m], sib_rs.at[m])
        xh_send[m] = (own[m, x_theirs, :] + sib_recv[m, x_theirs, :].astype(F32)).astype(BF16)
        send(xh_send.at[m], xh_recv.at[m], xh_ss.at[m], xh_rs.at[m], xhp)
        own[m, x_mine, :] = own[m, x_mine, :] + sib_recv[m, x_mine, :].astype(F32)

    for c in loads[6:8]:
        c.wait()
    scale = HD ** -0.5
    reach = [win_ref[0, 0], win_ref[0, 1]]

    def own_tile(t):
        r = pl.ds(t * TT, TT)
        blk = t // 2
        width = (t + 1) * TT
        s = dot_nt(q[r, :], k[pl.ds(0, width), :]) * scale
        qpos = lax.broadcasted_iota(jnp.int32, (TT, width), 0) + t * TT
        kpos = lax.broadcasted_iota(jnp.int32, (TT, width), 1)
        s = jnp.where(kpos <= qpos, s, MASKED)
        if blk == 1:
            far = jnp.where(reach[1] >= 1, 0.0, MASKED)
            s = s + jnp.where(kpos < BL, far, 0.0)
        top = jnp.max(s, axis=1, keepdims=True)
        p = jnp.exp(s - top)
        m_run[r, :] = top
        l_run[r, :] = jnp.sum(p, axis=1, keepdims=True)
        acc[r, :] = dot(p.astype(BF16), v[pl.ds(0, width), :])

    first = ctx == 0

    def halo_tile(t):
        r = pl.ds(t * TT, TT)
        blk = t // 2
        if blk == 0:
            lo, width = 0, HALO
        else:
            lo, width = BL, BL
        s = dot_nt(q[r, :], hk[pl.ds(lo, width), :]) * scale
        near = jnp.where(jnp.logical_or(reach[blk] < (1 if blk == 0 else 2), first), MASKED, 0.0)
        if blk == 0:
            far = jnp.where(jnp.logical_or(reach[blk] < 2, first), MASKED, 0.0)
            kpos = lax.broadcasted_iota(jnp.int32, (TT, width), 1)
            s = s + jnp.where(kpos < BL, far, near)
        else:
            s = s + near
        old = m_run[r, :]
        top = jnp.maximum(old, jnp.max(s, axis=1, keepdims=True))
        p = jnp.exp(s - top)
        keep = jnp.exp(old - top)
        total = l_run[r, :] * keep + jnp.sum(p, axis=1, keepdims=True)
        o = acc[r, :] * keep + dot(p.astype(BF16), hv[pl.ds(lo, width), :])
        acc[r, :] = o / total

    own_tile(0)
    own_tile(1)

    for m in range(3):
        arrived(xh_recv.at[m], xh_rs.at[m])
        red = own[m, x_mine, :] + xh_recv[m].astype(F32)
        own[m, x_mine, :] = red
        z_send[m] = red.astype(BF16)
        for d in range(1, NZ):
            dest = (z + d) % NZ
            send(
                z_send.at[m, pl.ds(pl.multiple_of(dest * SHARD, SHARD), SHARD)],
                z_recv.at[m, d - 1], z_ss.at[m, d - 1], z_rs.at[m, d - 1], zpeer[d],
            )

    own_tile(2)
    own_tile(3)

    base = core * HALF + xh * QUART
    z_mine = pl.ds(pl.multiple_of(xh * QUART + z * SHARD, SHARD), SHARD)
    for m in range(3):
        total = own[m, z_mine, :]
        for d in range(1, NZ):
            arrived(z_recv.at[m, d - 1], z_rs.at[m, d - 1])
            total = total + z_recv[m, d - 1].astype(F32)
        rows = pl.ds(pl.multiple_of(base + z * SHARD, SHARD), SHARD)
        gfull[m, rows, :] = total.astype(BF16)
        for d in range(1, NZ):
            send(gfull.at[m, rows], gfull.at[m, rows], ag_ss.at[m, d - 1], ag_rs.at[m, d - 1], zpeer[d])

    arrived(hk, halo_rs.at[0])
    arrived(hv, halo_rs.at[1])
    halo_tile(0)
    halo_tile(1)

    blk_z = pl.ds(pl.multiple_of(base, QUART), QUART)
    blk_x = pl.ds(pl.multiple_of(core * HALF + (1 - xh) * QUART, QUART), QUART)
    for m in range(3):
        for d in range(1, NZ):
            src = (z + NZ - d) % NZ
            rows = pl.ds(pl.multiple_of(base + src * SHARD, SHARD), SHARD)
            arrived(gfull.at[m, rows], ag_rs.at[m, d - 1])
        send(gfull.at[m, blk_z], gfull.at[m, blk_z], xg_ss.at[m], xg_rs.at[m], xhp)
        send(gfull.at[m, blk_z], gfull.at[m, blk_z], sg_ss.at[m, 0], sg_rs.at[m, 0], sib)

    halo_tile(2)
    halo_tile(3)

    for m in range(3):
        arrived(gfull.at[m, blk_x], xg_rs.at[m])
        send(gfull.at[m, blk_x], gfull.at[m, blk_x], sg_ss.at[m, 1], sg_rs.at[m, 1], sib)
    squares = jnp.zeros((1, HD), F32)
    for m in range(3):
        for j in range(2):
            half = pl.ds(
                pl.multiple_of((1 - core) * HALF + (xh if j == 0 else 1 - xh) * QUART, QUART), QUART
            )
            arrived(gfull.at[m, half], sg_rs.at[m, j])
        g = gfull[m].astype(F32)
        squares = squares + jnp.sum(g * g, axis=0, keepdims=True)

    gnorm = jnp.sqrt(jnp.sum(squares, axis=1, keepdims=True) + EPS)
    factor = jnp.minimum(1.0, GRAD_LIMIT / gnorm)
    for m, (old, new) in enumerate(((w2, n2), (w1, n1), (w3, n3))):
        w = old[0].astype(F32)
        u = w - factor * gfull[m].astype(F32)
        before = jnp.sqrt(jnp.sum(w * w, axis=0, keepdims=True) + EPS)
        after = jnp.sqrt(jnp.sum(u * u, axis=0, keepdims=True) + EPS)
        new[...] = (u * (before / after)).astype(BF16)

    def slot(h, t):
        return gat.at[h, pl.ds(t * GT, GT)]

    def pass_on(h, t, way):
        s = slot(h, t)
        if way == "x":
            send(s, s, gx_ss.at[t, h], g_rs.at[t, h], xp)
        elif way == "+":
            send(s, s, gy_ss.at[0, t, h], g_rs.at[t, h], yp)
        else:
            send(s, s, gy_ss.at[1, t, h], g_rs.at[t, h], ym)

    cols = [xl * 4 + (y + j) % NY for j in range(NY)]
    crss = [(1 - xl) * 4 + (y + j) % NY for j in range(NY)]

    for t in range(NT):
        r = pl.ds(t * TT, TT)
        qt = q[r, :]
        g = dot(qt, n1[...])
        u = dot(qt, n3[...])
        a = (g * sigmoid(g) * u).astype(BF16)
        f = dot(a, n2[...])
        ms = jnp.mean(f * f, axis=1, keepdims=True)
        nrm = f * lax.rsqrt(ms + EPS) * gain[...]
        gat[cols[0], r, :] = (nrm + acc[r, :]).astype(BF16)
        for tt in range(t * TT // GT, (t + 1) * TT // GT):
            for way in ("x", "+", "-"):
                pass_on(cols[0], tt, way)

    loads[8].wait()

    def got(h, t):
        arrived(slot(h, t), g_rs.at[t, h])

    for t in range(NG):
        if tile_kind(t) == "A":
            got(crss[0], t)
            pass_on(crss[0], t, "+")
            pass_on(crss[0], t, "-")
            got(cols[3], t)
            pass_on(cols[3], t, "+")
            got(cols[1], t)
            got(crss[1], t)
            pass_on(crss[1], t, "-")
            got(crss[3], t)
            got(cols[2], t)
            got(crss[2], t)
        else:
            plus = (t // 2) % 2 == 0
            got(cols[3], t)
            if plus:
                pass_on(cols[3], t, "+")
            pass_on(cols[3], t, "x")
            got(cols[1], t)
            if not plus:
                pass_on(cols[1], t, "-")
            pass_on(cols[1], t, "x")
            got(cols[2], t)
            pass_on(cols[2], t, "x")
            for j in (0, 3, 1, 2):
                got(crss[j], t)
        if (t + 1) * GT % TT == 0:
            r = pl.ds((t + 1) * GT - TT, TT)
            o = dot(gat[0, r, :], wo[pl.ds(0, HD), :])
            for h in range(1, HEADS):
                o = o + dot(gat[h, r, :], wo[pl.ds(h * HD, HD), :])
            outv[r, :] = o.astype(BF16)
            i = (t + 1) * GT // TT - 1
            pltpu.make_async_copy(outv.at[r], out_ref.at[r], out_sem.at[i]).start()

    for i in range(NT):
        r = pl.ds(i * TT, TT)
        pltpu.make_async_copy(outv.at[r], out_ref.at[r], out_sem.at[i]).wait()
    for c in sends:
        c.wait_send()


def per_device(*args):
    any_spec = pl.BlockSpec(memory_space=pl.ANY)
    in_specs = [any_spec] * 10
    in_specs[4] = pl.BlockSpec(memory_space=pltpu.SMEM)
    V = pltpu.VMEM
    D = pltpu.SemaphoreType.DMA
    scratch = [
        V((TOK, HD), BF16), V((TOK, HD), BF16), V((TOK, HD), BF16),
        V((HALO, HD), BF16), V((HALO, HD), BF16),
        V((1, HD, HD), BF16), V((1, HD, HD), BF16), V((1, HD, HD), BF16),
        V((HEADS * HD, COLS), BF16), V((1, TOK), F32), V((1, HD), F32),
        V((TOK, HD), BF16), V((TOK, HD), BF16), V((TOK, HD), BF16), V((TOK, HD), BF16),
        V((3, HALF, HD), BF16), V((3, HALF, HD), BF16), V((3, HALF, HD), F32),
        V((3, QUART, HD), BF16), V((3, QUART, HD), BF16),
        V((3, QUART, HD), BF16), V((3, NZ - 1, SHARD, HD), BF16), V((3, HD, HD), BF16),
        V((HD, HD), BF16), V((HD, HD), BF16), V((HD, HD), BF16),
        V((TOK, 1), F32), V((TOK, 1), F32), V((TOK, HD), F32),
        V((HEADS, TOK, HD), BF16), V((TOK, COLS), BF16),
        D((9,)), D((NT,)), D((2,)), D((2,)), D((3,)), D((3,)), D((3,)), D((3,)),
        D((3, NZ - 1)), D((3, NZ - 1)), D((3, NZ - 1)), D((3, NZ - 1)),
        D((3,)), D((3,)), D((3, 2)), D((3, 2)),
        D((2, NG, HEADS)), D((NG, HEADS)), D((NG, HEADS)),
    ]
    return pl.pallas_call(
        body,
        out_shape=jax.ShapeDtypeStruct((TOK, COLS), BF16),
        in_specs=in_specs,
        out_specs=any_spec,
        scratch_shapes=scratch,
        compiler_params=pltpu.CompilerParams(
            collective_id=0, has_side_effects=True, vmem_limit_bytes=60 << 20
        ),
        cost_estimate=pl.CostEstimate(flops=13_400_000_000, bytes_accessed=15_000_000, transcendentals=3_000_000),
        name="ttt_layer",
    )(*args)


def solution(mesh):
    placed = (
        P("ctx", "head"),
        P("ctx", "head"),
        P("ctx", "head"),
        P("head", "ctx"),
        P("head", "ctx"),
        P("head", None, None),
        P("head", None, None),
        P("head", None, None),
        P("head", None),
        P(None, "head"),
    )
    return jax.shard_map(
        per_device, mesh=mesh, in_specs=placed, out_specs=P("ctx", "head"), check_vma=False
    )
```

time: 435 us -> 171 us (0.39)
  the two profiles are of different devices: /device:TPU:2 before, /device:TPU:20 now
where the time goes in v1:
time: 171 us
  Pallas kernels  169 us (99%)
  local copies, waits for them, and re-layouts  2.49 us (1%)
    pallas_call x1, Pallas kernels, per_device(): pl.pallas_call(body, out_shape=jax.ShapeDtypeStruct((TOK, COLS), BF16), i...  169 us

profile of v1, /device:TPU:20, one launch (start us, length us, event | category | flops | bytes accessed | tf_op | source)
XLA Modules:
  0.0 171.2 jit_solution(8647618581582798044)
XLA Ops:
  0.0 168.7 %ttt_layer.1 = bf16[1024,640]{1,0:T(8,128)(2,1)} custom-call(bf16[1024,512]{1,0:T(8,128)(2,1)} %q_ref.1, bf16[1024,512]{1,0:T(8,128)(2,1)} %k_ref.1, bf16[1024,512]{1,0:T(8,128)(2,1)} %v_ref.1, f32[1,1024]{1,0:T(1,128)} %rate_ref.1, s32[1,2]{1,0:T(1,128)} %win_ref.1, bf16[1,512,512]{2,1,0:T(8,128)(2,1)} %w1_ref.1, bf16[1,512,512]{2,1,0:T(8,128)(2,1)} %w3_ref.1, ...), custom_call_target="tpu_custom_call" | custom-call | flops 13400000512 | bytes 15000000 | tf_op jit(solution)/shard_map/ttt_layer/pallas_call | solution.py:378
  168.7 2.5 %copy.12 = bf16[1024,640]{1,0:T(8,128)(2,1)} copy(bf16[1024,640]{1,0:T(8,128)(2,1)} %ttt_layer.1) | data formatting | bytes 2621440

commit v2 on v1

--- a/solution.py
+++ b/solution.py
@@ -18,12 +18,13 @@
 HEADS = 8
 COLS = 640
 HALF = 256
-QUART = 128
-SHARD = 16
+SHARD = 32
+HOPS = NZ // 2
 TT = 256
 NT = TOK // TT
 GT = 128
 NG = TOK // GT
+HP = 128
 GRAD_LIMIT = 24.0
 EPS = 1e-6
 MASKED = -1e30
@@ -43,6 +44,10 @@
 
 def dot_tn(a, b):
     return lax.dot_general(a, b, (((0,), (0,)), ((), ())), preferred_element_type=F32)
+
+
+def far_way(m):
+    return m % 2
 
 
 def tile_kind(t):
@@ -54,10 +59,10 @@
     out_ref,
     q, k, v, hk, hv, w1, w3, w2, wo, rate, gain,
     hid, tgt, bg, bu,
-    sib_send, sib_recv, own, xh_send, xh_recv, z_send, z_recv, gfull,
+    sib_send, sib_recv, own, rs_send, rs_recv, x_send, x_recv, gfull,
     n1, n3, n2, m_run, l_run, acc, gat, outv,
-    load_sem, out_sem, halo_ss, halo_rs, sib_ss, sib_rs, xh_ss, xh_rs, z_ss, z_rs,
-    ag_ss, ag_rs, xg_ss, xg_rs, sg_ss, sg_rs, gy_ss, gx_ss, g_rs,
+    load_sem, out_sem, halo_ss, halo_rs, sib_ss, sib_rs, rs_ss, rs_rs, x_ss, x_rs,
+    ag_ss, ag_rs, sg_ss, sg_rs, gy_ss, gx_ss, g_rs,
 ):
     ctx = lax.axis_index("ctx")
     head = lax.axis_index("head")
@@ -75,7 +80,7 @@
 
     sib = at_ctx(z, xh, 1 - core)
     xhp = at_ctx(z, 1 - xh, core)
-    zpeer = [None] + [at_ctx((z + d) % NZ, xh, core) for d in range(1, NZ)]
+    zway = (at_ctx((z + 1) % NZ, xh, core), at_ctx((z + NZ - 1) % NZ, xh, core))
     nxt = ((ctx + 1) % 32, head)
     prv = ((ctx + 31) % 32, head)
     xp = at_head(1 - xl, y)
@@ -83,7 +88,7 @@
     ym = at_head(xl, (y + 3) % NY)
 
     bar = pltpu.get_barrier_semaphore()
-    partners = [sib, xhp] + zpeer[1:] + [xp, yp, ym, prv]
+    partners = [sib, xhp, zway[0], zway[1], xp, yp, ym, prv]
     for p in partners:
         pl.semaphore_signal(bar, inc=1, device_id=p, device_id_type=MESH)
 
@@ -96,8 +101,6 @@
         c.start()
         loads.append(c)
 
-    pl.semaphore_wait(bar, len(partners))
-
     sends = []
 
     def send(src, dst, ss, rs, dev):
@@ -113,8 +116,26 @@
             src_ref=dst, dst_ref=dst, send_sem=rs, recv_sem=rs, device_id=sib, device_id_type=MESH
         ).wait_recv()
 
-    send(k_ref, hk, halo_ss.at[0], halo_rs.at[0], nxt)
-    send(v_ref, hv, halo_ss.at[1], halo_rs.at[1], nxt)
+    pieces = [
+        (src, dst, blk * BL + i * HP)
+        for blk in (1, 0)
+        for src, dst in ((k_ref, hk), (v_ref, hv))
+        for i in range(BL // HP)
+    ]
+    pushed = []
+
+    def push(count):
+        for _ in range(count):
+            i = len(pushed)
+            src, dst, lo = pieces[i]
+            pushed.append(i)
+            r = pl.ds(lo, HP)
+            send(src.at[r], dst.at[r], halo_ss.at[i], halo_rs.at[i], nxt)
+
+    def pulled(lo, hi):
+        for i in range(lo, hi):
+            src, dst, row = pieces[i]
+            arrived(dst.at[pl.ds(row, HP)], halo_rs.at[i])
 
     for c in loads[:6]:
         c.wait()
@@ -140,6 +161,8 @@
         return carry
 
     lax.fori_loop(0, NT, grad_tile, 0)
+    pl.semaphore_wait(bar, len(partners))
+    push(5)
 
     theirs = pl.ds(pl.multiple_of((1 - core) * HALF, HALF), HALF)
     mine = pl.ds(pl.multiple_of(core * HALF, HALF), HALF)
@@ -150,13 +173,9 @@
     for m, (a, b) in enumerate(pairs):
         own[m] = dot_tn(a[:, mine], b[...])
 
-    x_theirs = pl.ds(pl.multiple_of((1 - xh) * QUART, QUART), QUART)
-    x_mine = pl.ds(pl.multiple_of(xh * QUART, QUART), QUART)
     for m in range(3):
         arrived(sib_recv.at[m], sib_rs.at[m])
-        xh_send[m] = (own[m, x_theirs, :] + sib_recv[m, x_theirs, :].astype(F32)).astype(BF16)
-        send(xh_send.at[m], xh_recv.at[m], xh_ss.at[m], xh_rs.at[m], xhp)
-        own[m, x_mine, :] = own[m, x_mine, :] + sib_recv[m, x_mine, :].astype(F32)
+        own[m] = own[m] + sib_recv[m].astype(F32)
 
     for c in loads[6:8]:
         c.wait()
@@ -205,64 +224,80 @@
         o = acc[r, :] * keep + dot(p.astype(BF16), hv[pl.ds(lo, width), :])
         acc[r, :] = o / total
 
-    own_tile(0)
-    own_tile(1)
+    def shard(d):
+        return pl.ds(pl.multiple_of(((z + NZ + d) % NZ) * SHARD, SHARD), SHARD)
+
+    def goes(m, way, step):
+        return step > 1 or far_way(m) == way
+
+    for step in range(1, HOPS + 1):
+        for m in range(3):
+            for way in range(2):
+                if not goes(m, way, step):
+                    continue
+                dist = HOPS + 1 - step
+                part = own[m, shard(dist if way == 0 else -dist), :]
+                if step > 1 and goes(m, way, step - 1):
+                    arrived(rs_recv.at[m, way, step - 2], rs_rs.at[m, way, step - 2])
+                    part = part + rs_recv[m, way, step - 2].astype(F32)
+                rs_send[m, way, step - 1] = part.astype(BF16)
+                send(
+                    rs_send.at[m, way, step - 1], rs_recv.at[m, way, step - 1],
+                    rs_ss.at[m, way, step - 1], rs_rs.at[m, way, step - 1], zway[way],
+                )
+        push(1)
+        own_tile(step - 1)
 
     for m in range(3):
-        arrived(xh_recv.at[m], xh_rs.at[m])
-        red = own[m, x_mine, :] + xh_recv[m].astype(F32)
-        own[m, x_mine, :] = red
-        z_send[m] = red.astype(BF16)
-        for d in range(1, NZ):
-            dest = (z + d) % NZ
-            send(
-                z_send.at[m, pl.ds(pl.multiple_of(dest * SHARD, SHARD), SHARD)],
-                z_recv.at[m, d - 1], z_ss.at[m, d - 1], z_rs.at[m, d - 1], zpeer[d],
-            )
-
-    own_tile(2)
-    own_tile(3)
-
-    base = core * HALF + xh * QUART
-    z_mine = pl.ds(pl.multiple_of(xh * QUART + z * SHARD, SHARD), SHARD)
+        part = own[m, shard(0), :]
+        for way in range(2):
+            arrived(rs_recv.at[m, way, HOPS - 1], rs_rs.at[m, way, HOPS - 1])
+            part = part + rs_recv[m, way, HOPS - 1].astype(F32)
+        x_send[m] = part.astype(BF16)
+        send(x_send.at[m], x_recv.at[m], x_ss.at[m], x_rs.at[m], xhp)
+    push(2)
+
+    def rows_of(d, cc):
+        return pl.ds(pl.multiple_of(cc * HALF + ((z + NZ + d) % NZ) * SHARD, SHARD), SHARD)
+
+    def to_ring(m, d, way, dist):
+        r = gfull.at[m, rows_of(d, core)]
+        send(r, r, ag_ss.at[m, way, dist - 1], ag_rs.at[m, way, dist - 1], zway[way])
+
+    def to_core(m, d):
+        r = gfull.at[m, rows_of(d, core)]
+        i = d % NZ
+        send(r, r, sg_ss.at[m, i], sg_rs.at[m, i], sib)
+
     for m in range(3):
-        total = own[m, z_mine, :]
-        for d in range(1, NZ):
-            arrived(z_recv.at[m, d - 1], z_rs.at[m, d - 1])
-            total = total + z_recv[m, d - 1].astype(F32)
-        rows = pl.ds(pl.multiple_of(base + z * SHARD, SHARD), SHARD)
-        gfull[m, rows, :] = total.astype(BF16)
-        for d in range(1, NZ):
-            send(gfull.at[m, rows], gfull.at[m, rows], ag_ss.at[m, d - 1], ag_rs.at[m, d - 1], zpeer[d])
-
-    arrived(hk, halo_rs.at[0])
-    arrived(hv, halo_rs.at[1])
-    halo_tile(0)
-    halo_tile(1)
-
-    blk_z = pl.ds(pl.multiple_of(base, QUART), QUART)
-    blk_x = pl.ds(pl.multiple_of(core * HALF + (1 - xh) * QUART, QUART), QUART)
-    for m in range(3):
-        for d in range(1, NZ):
-            src = (z + NZ - d) % NZ
-            rows = pl.ds(pl.multiple_of(base + src * SHARD, SHARD), SHARD)
-            arrived(gfull.at[m, rows], ag_rs.at[m, d - 1])
-        send(gfull.at[m, blk_z], gfull.at[m, blk_z], xg_ss.at[m], xg_rs.at[m], xhp)
-        send(gfull.at[m, blk_z], gfull.at[m, blk_z], sg_ss.at[m, 0], sg_rs.at[m, 0], sib)
-
-    halo_tile(2)
-    halo_tile(3)
-
-    for m in range(3):
-        arrived(gfull.at[m, blk_x], xg_rs.at[m])
-        send(gfull.at[m, blk_x], gfull.at[m, blk_x], sg_ss.at[m, 1], sg_rs.at[m, 1], sib)
+        arrived(x_recv.at[m], x_rs.at[m])
+        both = x_send[m].astype(F32) + x_recv[m].astype(F32)
+        gfull[m, rows_of(0, core), :] = both.astype(BF16)
+        to_ring(m, 0, 0, 1)
+        to_ring(m, 0, 1, 1)
+        to_core(m, 0)
+
+    for dist in range(1, HOPS + 1):
+        for m in range(3):
+            for way in range(2):
+                if dist == HOPS and far_way(m) != way:
+                    continue
+                d = -dist if way == 0 else dist
+                arrived(gfull.at[m, rows_of(d, core)], ag_rs.at[m, way, dist - 1])
+                if dist + 1 < HOPS or (dist + 1 == HOPS and far_way(m) == way):
+                    to_ring(m, d, way, dist + 1)
+                to_core(m, d)
+        if dist < HOPS:
+            push((2, 2, 1)[dist - 1])
+
+    pulled(0, len(pieces))
+    for t in range(NT):
+        halo_tile(t)
+
     squares = jnp.zeros((1, HD), F32)
     for m in range(3):
-        for j in range(2):
-            half = pl.ds(
-                pl.multiple_of((1 - core) * HALF + (xh if j == 0 else 1 - xh) * QUART, QUART), QUART
-            )
-            arrived(gfull.at[m, half], sg_rs.at[m, j])
+        for d in range(NZ):
+            arrived(gfull.at[m, rows_of(d, 1 - core)], sg_rs.at[m, d])
         g = gfull[m].astype(F32)
         squares = squares + jnp.sum(g * g, axis=0, keepdims=True)
 
@@ -290,7 +325,7 @@
     cols = [xl * 4 + (y + j) % NY for j in range(NY)]
     crss = [(1 - xl) * 4 + (y + j) % NY for j in range(NY)]
 
-    for t in range(NT):
+    def readout(t):
         r = pl.ds(t * TT, TT)
         qt = q[r, :]
         g = dot(qt, n1[...])
@@ -300,16 +335,15 @@
         ms = jnp.mean(f * f, axis=1, keepdims=True)
         nrm = f * lax.rsqrt(ms + EPS) * gain[...]
         gat[cols[0], r, :] = (nrm + acc[r, :]).astype(BF16)
-        for tt in range(t * TT // GT, (t + 1) * TT // GT):
-            for way in ("x", "+", "-"):
-                pass_on(cols[0], tt, way)
-
-    loads[8].wait()
 
     def got(h, t):
         arrived(slot(h, t), g_rs.at[t, h])
 
-    for t in range(NG):
+    def own_out(t):
+        for way in ("x", "+", "-"):
+            pass_on(cols[0], t, way)
+
+    def one_hop(t):
         if tile_kind(t) == "A":
             got(crss[0], t)
             pass_on(crss[0], t, "+")
@@ -317,11 +351,6 @@
             got(cols[3], t)
             pass_on(cols[3], t, "+")
             got(cols[1], t)
-            got(crss[1], t)
-            pass_on(crss[1], t, "-")
-            got(crss[3], t)
-            got(cols[2], t)
-            got(crss[2], t)
         else:
             plus = (t // 2) % 2 == 0
             got(cols[3], t)
@@ -332,18 +361,53 @@
             if not plus:
                 pass_on(cols[1], t, "-")
             pass_on(cols[1], t, "x")
+
+    def two_hops(t):
+        if tile_kind(t) == "A":
+            got(crss[1], t)
+            pass_on(crss[1], t, "-")
+            got(crss[3], t)
+            got(cols[2], t)
+        else:
             got(cols[2], t)
             pass_on(cols[2], t, "x")
-            for j in (0, 3, 1, 2):
+            got(crss[0], t)
+
+    def rest(t):
+        if tile_kind(t) == "A":
+            got(crss[2], t)
+        else:
+            for j in (3, 1, 2):
                 got(crss[j], t)
-        if (t + 1) * GT % TT == 0:
-            r = pl.ds((t + 1) * GT - TT, TT)
-            o = dot(gat[0, r, :], wo[pl.ds(0, HD), :])
-            for h in range(1, HEADS):
-                o = o + dot(gat[h, r, :], wo[pl.ds(h * HD, HD), :])
-            outv[r, :] = o.astype(BF16)
-            i = (t + 1) * GT // TT - 1
-            pltpu.make_async_copy(outv.at[r], out_ref.at[r], out_sem.at[i]).start()
+
+    def project(i):
+        r = pl.ds(i * TT, TT)
+        o = dot(gat[0, r, :], wo[pl.ds(0, HD), :])
+        for h in range(1, HEADS):
+            o = o + dot(gat[h, r, :], wo[pl.ds(h * HD, HD), :])
+        outv[r, :] = o.astype(BF16)
+        pltpu.make_async_copy(outv.at[r], out_ref.at[r], out_sem.at[i]).start()
+
+    PER = TT // GT
+    readout(0)
+    own_out(0)
+    readout(1)
+    own_out(1)
+    readout(2)
+    readout(3)
+    loads[8].wait()
+    for step in range(1, NG + 4):
+        if step - 1 < NG:
+            one_hop(step - 1)
+        if 0 <= step - 2 < NG:
+            two_hops(step - 2)
+        if step + 1 < NG:
+            own_out(step + 1)
+        if 0 <= step - 4 < NG:
+            t = step - 4
+            rest(t)
+            if (t + 1) % PER == 0:
+                project(t // PER)
 
     for i in range(NT):
         r = pl.ds(i * TT, TT)
@@ -365,14 +429,14 @@
         V((HEADS * HD, COLS), BF16), V((1, TOK), F32), V((1, HD), F32),
         V((TOK, HD), BF16), V((TOK, HD), BF16), V((TOK, HD), BF16), V((TOK, HD), BF16),
         V((3, HALF, HD), BF16), V((3, HALF, HD), BF16), V((3, HALF, HD), F32),
-        V((3, QUART, HD), BF16), V((3, QUART, HD), BF16),
-        V((3, QUART, HD), BF16), V((3, NZ - 1, SHARD, HD), BF16), V((3, HD, HD), BF16),
+        V((3, 2, HOPS, SHARD, HD), BF16), V((3, 2, HOPS, SHARD, HD), BF16),
+        V((3, SHARD, HD), BF16), V((3, SHARD, HD), BF16), V((3, HD, HD), BF16),
         V((HD, HD), BF16), V((HD, HD), BF16), V((HD, HD), BF16),
         V((TOK, 1), F32), V((TOK, 1), F32), V((TOK, HD), F32),
         V((HEADS, TOK, HD), BF16), V((TOK, COLS), BF16),
-        D((9,)), D((NT,)), D((2,)), D((2,)), D((3,)), D((3,)), D((3,)), D((3,)),
-        D((3, NZ - 1)), D((3, NZ - 1)), D((3, NZ - 1)), D((3, NZ - 1)),
-        D((3,)), D((3,)), D((3, 2)), D((3, 2)),
+        D((9,)), D((NT,)), D((16,)), D((16,)), D((3,)), D((3,)),
+        D((3, 2, HOPS)), D((3, 2, HOPS)), D((3,)), D((3,)),
+        D((3, 2, HOPS)), D((3, 2, HOPS)), D((3, NZ)), D((3, NZ)),
         D((2, NG, HEADS)), D((NG, HEADS)), D((NG, HEADS)),
     ]
     return pl.pallas_call(

time: 171 us -> 127 us (0.74)
  the two profiles are of different devices: /device:TPU:20 before, /device:TPU:4 now
where the time goes in v2:
time: 127 us
  Pallas kernels  124 us (98%)
  local copies, waits for them, and re-layouts  2.49 us (2%)
    pallas_call x1, Pallas kernels, per_device(): pl.pallas_call(body, out_shape=jax.ShapeDtypeStruct((TOK, COLS), BF16), i...  124 us

profile of v2, /device:TPU:4, one launch (start us, length us, event | category | flops | bytes accessed | tf_op | source)
XLA Modules:
  0.0 126.5 jit_solution(14467271653672103153)
XLA Ops:
  0.0 124.0 %ttt_layer.1 = bf16[1024,640]{1,0:T(8,128)(2,1)} custom-call(bf16[1024,512]{1,0:T(8,128)(2,1)} %q_ref.1, bf16[1024,512]{1,0:T(8,128)(2,1)} %k_ref.1, bf16[1024,512]{1,0:T(8,128)(2,1)} %v_ref.1, f32[1,1024]{1,0:T(1,128)} %rate_ref.1, s32[1,2]{1,0:T(1,128)} %win_ref.1, bf16[1,512,512]{2,1,0:T(8,128)(2,1)} %w1_ref.1, bf16[1,512,512]{2,1,0:T(8,128)(2,1)} %w3_ref.1, ...), custom_call_target="tpu_custom_call" | custom-call | flops 13400000512 | bytes 15000000 | tf_op jit(solution)/shard_map/ttt_layer/pallas_call | solution.py:442
  124.1 2.5 %copy.12 = bf16[1024,640]{1,0:T(8,128)(2,1)} copy(bf16[1024,640]{1,0:T(8,128)(2,1)} %ttt_layer.1) | data formatting | bytes 2621440

commit v3 on v2

--- a/solution.py
+++ b/solution.py
@@ -22,8 +22,12 @@
 HOPS = NZ // 2
 TT = 256
 NT = TOK // TT
-GT = 128
-NG = TOK // GT
+MY = TOK // 2
+GT = 64
+NG = MY // GT
+PT = 128
+NP = MY // PT
+WP = HEADS // 2
 HP = 128
 GRAD_LIMIT = 24.0
 EPS = 1e-6
@@ -50,19 +54,15 @@
     return m % 2
 
 
-def tile_kind(t):
-    return "A" if t % 2 == 0 else "B"
-
-
 def body(
     q_ref, k_ref, v_ref, rate_ref, win_ref, w1_ref, w3_ref, w2_ref, gain_ref, wo_ref,
     out_ref,
-    q, k, v, hk, hv, w1, w3, w2, wo, rate, gain,
+    q, k, v, hk, hv, stage, w1, w3, w2, wo, rate, gain,
     hid, tgt, bg, bu,
     sib_send, sib_recv, own, rs_send, rs_recv, x_send, x_recv, gfull,
-    n1, n3, n2, m_run, l_run, acc, gat, outv,
-    load_sem, out_sem, halo_ss, halo_rs, sib_ss, sib_rs, rs_ss, rs_rs, x_ss, x_rs,
-    ag_ss, ag_rs, sg_ss, sg_rs, gy_ss, gx_ss, g_rs,
+    n1, n3, n2, m_run, l_run, acc, gat, oth, wo2, sum_here, sum_pair, opair, outv,
+    load_sem, out_sem, halo_ss, halo_rs, stage_ss, stage_rs, sib_ss, sib_rs, rs_ss, rs_rs, x_ss, x_rs,
+    ag_ss, ag_rs, sg_ss, sg_rs, g_ss, g_rs, w_ss, w_rs, ws_ss, ws_rs, o_ss, o_rs,
 ):
     ctx = lax.axis_index("ctx")
     head = lax.axis_index("head")
@@ -83,12 +83,20 @@
     zway = (at_ctx((z + 1) % NZ, xh, core), at_ctx((z + NZ - 1) % NZ, xh, core))
     nxt = ((ctx + 1) % 32, head)
     prv = ((ctx + 31) % 32, head)
+    over = at_ctx((z + 1) % NZ, xh, 1 - core)
+    under = at_ctx((z + NZ - 1) % NZ, xh, 1 - core)
+    crosses = jnp.logical_and(core == 1, xh == 1)
+    relays = jnp.logical_and(core == 1, xh == 0)
     xp = at_head(1 - xl, y)
-    yp = at_head(xl, (y + 1) % NY)
-    ym = at_head(xl, (y + 3) % NY)
+    group = y // 2
+    y_pair = 3 - y
+    y_mate = 1 - y + 4 * group
+    y_far = 3 - y_mate
+    pair = at_head(xl, y_pair)
+    mate = at_head(xl, y_mate)
 
     bar = pltpu.get_barrier_semaphore()
-    partners = [sib, xhp, zway[0], zway[1], xp, yp, ym, prv]
+    partners = [sib, xhp, zway[0], zway[1], xp, pair, mate, prv, under]
     for p in partners:
         pl.semaphore_signal(bar, inc=1, device_id=p, device_id_type=MESH)
 
@@ -98,15 +106,19 @@
          (q_ref, q), (gain_ref, gain), (wo_ref, wo))
     ):
         c = pltpu.make_async_copy(src, dst, load_sem.at[i])
-        c.start()
+        if i < 6:
+            c.start()
         loads.append(c)
 
     sends = []
 
-    def send(src, dst, ss, rs, dev):
-        c = pltpu.make_async_remote_copy(
+    def copy(src, dst, ss, rs, dev):
+        return pltpu.make_async_remote_copy(
             src_ref=src, dst_ref=dst, send_sem=ss, recv_sem=rs, device_id=dev, device_id_type=MESH
         )
+
+    def send(src, dst, ss, rs, dev):
+        c = copy(src, dst, ss, rs, dev)
         c.start()
         sends.append(c)
         return c
@@ -119,10 +131,11 @@
     pieces = [
         (src, dst, blk * BL + i * HP)
         for blk in (1, 0)
-        for src, dst in ((k_ref, hk), (v_ref, hv))
         for i in range(BL // HP)
+        for src, dst in ((v_ref, hv), (k_ref, hk))
     ]
     pushed = []
+    passed = []
 
     def push(count):
         for _ in range(count):
@@ -130,7 +143,34 @@
             src, dst, lo = pieces[i]
             pushed.append(i)
             r = pl.ds(lo, HP)
-            send(src.at[r], dst.at[r], halo_ss.at[i], halo_rs.at[i], nxt)
+            if dst is hk:
+                send(src.at[r], dst.at[r], halo_ss.at[i], halo_rs.at[i], nxt)
+                continue
+
+            c = copy(src.at[r], dst.at[r], halo_ss.at[i], halo_rs.at[i], nxt)
+            first_leg = copy(src.at[r], stage.at[r], halo_ss.at[i], stage_rs.at[i], xhp)
+            sends.append(c)
+
+            @pl.when(jnp.logical_not(crosses))
+            def _():
+                c.start()
+
+            @pl.when(crosses)
+            def _():
+                first_leg.start()
+
+    def pass_values(count):
+        for _ in range(count):
+            i = 2 * len(passed)
+            src, dst, lo = pieces[i]
+            r = pl.ds(lo, HP)
+            c = copy(stage.at[r], dst.at[r], stage_ss.at[i], halo_rs.at[i], over)
+            passed.append(c)
+
+            @pl.when(relays)
+            def _():
+                arrived(stage.at[r], stage_rs.at[i])
+                c.start()
 
     def pulled(lo, hi):
         for i in range(lo, hi):
@@ -139,6 +179,8 @@
 
     for c in loads[:6]:
         c.wait()
+    for c in loads[6:]:
+        c.start()
 
     def grad_tile(t, carry):
         r = pl.ds(pl.multiple_of(t * TT, TT), TT)
@@ -160,9 +202,25 @@
         bu[r, :] = (ba * sv).astype(BF16)
         return carry
 
-    lax.fori_loop(0, NT, grad_tile, 0)
+    lax.fori_loop(0, 2, grad_tile, 0)
     pl.semaphore_wait(bar, len(partners))
-    push(5)
+    push(6)
+
+    def w_rows(cc, i):
+        return pl.ds(pl.multiple_of((cc * WP + i) * HD, HD), HD)
+
+    for i in range(WP):
+        r = w_rows(core, i)
+        send(wo_ref.at[r], wo2.at[r], w_ss.at[i], w_rs.at[i], pair)
+
+    lax.fori_loop(2, NT, grad_tile, 0)
+    push(3)
+
+    def w_on(i):
+        r = wo2.at[w_rows(core, i)]
+        arrived(r, w_rs.at[i])
+        send(r, r, ws_ss.at[i], ws_rs.at[i], sib)
+
 
     theirs = pl.ds(pl.multiple_of((1 - core) * HALF, HALF), HALF)
     mine = pl.ds(pl.multiple_of(core * HALF, HALF), HALF)
@@ -246,6 +304,7 @@
                     rs_ss.at[m, way, step - 1], rs_rs.at[m, way, step - 1], zway[way],
                 )
         push(1)
+        pass_values(2 if step == 1 else 1)
         own_tile(step - 1)
 
     for m in range(3):
@@ -256,6 +315,7 @@
         x_send[m] = part.astype(BF16)
         send(x_send.at[m], x_recv.at[m], x_ss.at[m], x_rs.at[m], xhp)
     push(2)
+    pass_values(1)
 
     def rows_of(d, cc):
         return pl.ds(pl.multiple_of(cc * HALF + ((z + NZ + d) % NZ) * SHARD, SHARD), SHARD)
@@ -287,9 +347,12 @@
                 if dist + 1 < HOPS or (dist + 1 == HOPS and far_way(m) == way):
                     to_ring(m, d, way, dist + 1)
                 to_core(m, d)
-        if dist < HOPS:
-            push((2, 2, 1)[dist - 1])
-
+        if dist < 3:
+            push(2 - dist)
+            pass_values(1)
+
+    w_on(0)
+    w_on(1)
     pulled(0, len(pieces))
     for t in range(NT):
         halo_tile(t)
@@ -310,23 +373,17 @@
         after = jnp.sqrt(jnp.sum(u * u, axis=0, keepdims=True) + EPS)
         new[...] = (u * (before / after)).astype(BF16)
 
-    def slot(h, t):
-        return gat.at[h, pl.ds(t * GT, GT)]
-
-    def pass_on(h, t, way):
-        s = slot(h, t)
-        if way == "x":
-            send(s, s, gx_ss.at[t, h], g_rs.at[t, h], xp)
-        elif way == "+":
-            send(s, s, gy_ss.at[0, t, h], g_rs.at[t, h], yp)
-        else:
-            send(s, s, gy_ss.at[1, t, h], g_rs.at[t, h], ym)
-
-    cols = [xl * 4 + (y + j) % NY for j in range(NY)]
-    crss = [(1 - xl) * 4 + (y + j) % NY for j in range(NY)]
-
-    def readout(t):
-        r = pl.ds(t * TT, TT)
+    h_own = head
+    h_mate = xl * 4 + y_mate
+    h_pair = xl * 4 + y_pair
+    h_far = xl * 4 + y_far
+    x_own = (1 - xl) * 4 + y
+    x_mate = (1 - xl) * 4 + y_mate
+    x_pair = (1 - xl) * 4 + y_pair
+    x_far = (1 - xl) * 4 + y_far
+
+    def readout(half, i):
+        r = pl.ds(pl.multiple_of(half * MY + i * TT, TT), TT)
         qt = q[r, :]
         g = dot(qt, n1[...])
         u = dot(qt, n3[...])
@@ -334,86 +391,143 @@
         f = dot(a, n2[...])
         ms = jnp.mean(f * f, axis=1, keepdims=True)
         nrm = f * lax.rsqrt(ms + EPS) * gain[...]
-        gat[cols[0], r, :] = (nrm + acc[r, :]).astype(BF16)
+        return (nrm + acc[r, :]).astype(BF16)
+
+    def slot(h, t):
+        return gat.at[h, pl.ds(t * GT, GT)]
 
     def got(h, t):
         arrived(slot(h, t), g_rs.at[t, h])
 
+    def pass_on(h, t, kind, dev):
+        send(slot(h, t), slot(h, t), g_ss.at[t, kind], g_rs.at[t, h], dev)
+
     def own_out(t):
-        for way in ("x", "+", "-"):
-            pass_on(cols[0], t, way)
-
-    def one_hop(t):
-        if tile_kind(t) == "A":
-            got(crss[0], t)
-            pass_on(crss[0], t, "+")
-            pass_on(crss[0], t, "-")
-            got(cols[3], t)
-            pass_on(cols[3], t, "+")
-            got(cols[1], t)
+        pass_on(h_own, t, 0, xp)
+        pass_on(h_own, t, 1, mate)
+
+    def other_out(t):
+        send(oth.at[pl.ds(t * GT, GT)], slot(h_own, t), g_ss.at[t, 2], g_rs.at[t, h_own], pair)
+
+    def near_one(t):
+        if t % 2 == 0:
+            got(x_own, t)
+            pass_on(x_own, t, 3, mate)
         else:
-            plus = (t // 2) % 2 == 0
-            got(cols[3], t)
-            if plus:
-                pass_on(cols[3], t, "+")
-            pass_on(cols[3], t, "x")
-            got(cols[1], t)
-            if not plus:
-                pass_on(cols[1], t, "-")
-            pass_on(cols[1], t, "x")
-
-    def two_hops(t):
-        if tile_kind(t) == "A":
-            got(crss[1], t)
-            pass_on(crss[1], t, "-")
-            got(crss[3], t)
-            got(cols[2], t)
+            got(h_mate, t)
+            pass_on(h_mate, t, 3, xp)
+
+    def near_rest(t):
+        got(h_mate if t % 2 == 0 else x_own, t)
+        got(x_mate, t)
+
+    def pair_one(t):
+        got(h_pair, t)
+        pass_on(h_pair, t, 4, mate)
+        pass_on(h_pair, t, 5, xp)
+
+    def pair_two(t):
+        if t % 2 == 0:
+            got(h_far, t)
+            pass_on(h_far, t, 6, xp)
         else:
-            got(cols[2], t)
-            pass_on(cols[2], t, "x")
-            got(crss[0], t)
-
-    def rest(t):
-        if tile_kind(t) == "A":
-            got(crss[2], t)
-        else:
-            for j in (3, 1, 2):
-                got(crss[j], t)
+            got(x_pair, t)
+            pass_on(x_pair, t, 6, mate)
+
+    def pair_rest(t):
+        got(x_pair if t % 2 == 0 else h_far, t)
+        got(x_far, t)
+
+    def heads_dot(heads, r, w):
+        o = None
+        for h in heads:
+            p = dot(gat[h, r, :], w[pl.ds(pl.multiple_of(h * HD, HD), HD), :])
+            o = p if o is None else o + p
+        return o
+
+    near = (h_own, h_mate, x_own, x_mate)
+    distant = (h_pair, h_far, x_pair, x_far)
 
     def project(i):
+        r = pl.ds(i * PT, PT)
+        here = pl.ds(pl.multiple_of(group * MY + i * PT, PT), PT)
+        opair[r, :] = (sum_pair[r, :] + heads_dot(distant, r, wo2)).astype(BF16)
+        send(opair.at[r], outv.at[here], o_ss.at[i], o_rs.at[i], pair)
+        outv[here, :] = (sum_here[r, :] + heads_dot(distant, r, wo)).astype(BF16)
+        pltpu.make_async_copy(outv.at[here], out_ref.at[here], out_sem.at[0, i]).start()
+
+    for i in range(MY // TT):
         r = pl.ds(i * TT, TT)
-        o = dot(gat[0, r, :], wo[pl.ds(0, HD), :])
-        for h in range(1, HEADS):
-            o = o + dot(gat[h, r, :], wo[pl.ds(h * HD, HD), :])
-        outv[r, :] = o.astype(BF16)
-        pltpu.make_async_copy(outv.at[r], out_ref.at[r], out_sem.at[i]).start()
-
-    PER = TT // GT
-    readout(0)
-    own_out(0)
-    readout(1)
-    own_out(1)
-    readout(2)
-    readout(3)
+        gat[h_own, r, :] = readout(group, i)
+        for t in range(i * TT // GT, (i + 1) * TT // GT):
+            own_out(t)
+        oth[r, :] = readout(1 - group, i)
+        for t in range(i * TT // GT, (i + 1) * TT // GT):
+            other_out(t)
+    w_on(2)
     loads[8].wait()
-    for step in range(1, NG + 4):
-        if step - 1 < NG:
-            one_hop(step - 1)
-        if 0 <= step - 2 < NG:
-            two_hops(step - 2)
-        if step + 1 < NG:
-            own_out(step + 1)
-        if 0 <= step - 4 < NG:
-            t = step - 4
-            rest(t)
-            if (t + 1) % PER == 0:
-                project(t // PER)
-
-    for i in range(NT):
+
+    def sum_up(i):
         r = pl.ds(i * TT, TT)
-        pltpu.make_async_copy(outv.at[r], out_ref.at[r], out_sem.at[i]).wait()
+        sum_here[r, :] = heads_dot(near, r, wo)
+
+    def sum_up_pair(i):
+        r = pl.ds(i * TT, TT)
+        sum_pair[r, :] = heads_dot(near, r, wo2)
+
+    for t in range(NG):
+        near_one(t)
+    w_on(3)
+    for t in (0, 1):
+        pair_one(t)
+    for t in range(4):
+        near_rest(t)
+    sum_up(0)
+    for t in (2, 3):
+        pair_one(t)
+    for t in (0, 1):
+        pair_two(t)
+    for t in range(4, 8):
+        near_rest(t)
+    sum_up(1)
+    for t in (4, 5):
+        pair_one(t)
+    for t in (2, 3):
+        pair_two(t)
+    for i in range(WP):
+        arrived(wo2.at[w_rows(1 - core, i)], ws_rs.at[i])
+    sum_up_pair(0)
+    for t in (6, 7):
+        pair_one(t)
+    for t in (4, 5):
+        pair_two(t)
+    sum_up_pair(1)
+    for t in (0, 1):
+        pair_rest(t)
+    project(0)
+    for t in (6, 7):
+        pair_two(t)
+    for i in range(1, NP):
+        for t in (2 * i, 2 * i + 1):
+            pair_rest(t)
+        project(i)
+
+    for i in range(NP):
+        there = pl.ds(pl.multiple_of((1 - group) * MY + i * PT, PT), PT)
+        arrived(outv.at[there], o_rs.at[i])
+        pltpu.make_async_copy(outv.at[there], out_ref.at[there], out_sem.at[1, i]).start()
+    for i in range(NP):
+        for j in range(2):
+            half = group if j == 0 else 1 - group
+            r = pl.ds(pl.multiple_of(half * MY + i * PT, PT), PT)
+            pltpu.make_async_copy(outv.at[r], out_ref.at[r], out_sem.at[j, i]).wait()
     for c in sends:
         c.wait_send()
+
+    @pl.when(relays)
+    def _():
+        for c in passed:
+            c.wait_send()
 
 
 def per_device(*args):
@@ -424,7 +538,7 @@
     D = pltpu.SemaphoreType.DMA
     scratch = [
         V((TOK, HD), BF16), V((TOK, HD), BF16), V((TOK, HD), BF16),
-        V((HALO, HD), BF16), V((HALO, HD), BF16),
+        V((HALO, HD), BF16), V((HALO, HD), BF16), V((HALO, HD), BF16),
         V((1, HD, HD), BF16), V((1, HD, HD), BF16), V((1, HD, HD), BF16),
         V((HEADS * HD, COLS), BF16), V((1, TOK), F32), V((1, HD), F32),
         V((TOK, HD), BF16), V((TOK, HD), BF16), V((TOK, HD), BF16), V((TOK, HD), BF16),
@@ -433,11 +547,13 @@
         V((3, SHARD, HD), BF16), V((3, SHARD, HD), BF16), V((3, HD, HD), BF16),
         V((HD, HD), BF16), V((HD, HD), BF16), V((HD, HD), BF16),
         V((TOK, 1), F32), V((TOK, 1), F32), V((TOK, HD), F32),
-        V((HEADS, TOK, HD), BF16), V((TOK, COLS), BF16),
-        D((9,)), D((NT,)), D((16,)), D((16,)), D((3,)), D((3,)),
+        V((HEADS, MY, HD), BF16), V((MY, HD), BF16),
+        V((HEADS * HD, COLS), BF16), V((MY, COLS), F32), V((MY, COLS), F32),
+        V((MY, COLS), BF16), V((TOK, COLS), BF16),
+        D((9,)), D((2, NP)), D((16,)), D((16,)), D((16,)), D((16,)), D((3,)), D((3,)),
         D((3, 2, HOPS)), D((3, 2, HOPS)), D((3,)), D((3,)),
         D((3, 2, HOPS)), D((3, 2, HOPS)), D((3, NZ)), D((3, NZ)),
-        D((2, NG, HEADS)), D((NG, HEADS)), D((NG, HEADS)),
+        D((NG, 7)), D((NG, HEADS)), D((WP,)), D((WP,)), D((WP,)), D((WP,)), D((NP,)), D((NP,)),
     ]
     return pl.pallas_call(
         body,

time: 127 us -> 107 us (0.84)
  the two profiles are of different devices: /device:TPU:4 before, /device:TPU:2 now
where the time goes in v3:
time: 107 us
  Pallas kernels  105 us (98%)
  local copies, waits for them, and re-layouts  2.49 us (2%)
    pallas_call x1, Pallas kernels, per_device(): pl.pallas_call(body, out_shape=jax.ShapeDtypeStruct((TOK, COLS), BF16), i...  105 us
    unnamed x1, local copies, waits for them, and re-layouts  2.49 us

profile of v3, /device:TPU:2, one launch (start us, length us, event | category | flops | bytes accessed | tf_op | source)
XLA Modules:
  0.0 107.2 jit_solution(7054665305630777298)
XLA Ops:
  0.0 104.7 %ttt_layer.1 = bf16[1024,640]{1,0:T(8,128)(2,1)} custom-call(bf16[1024,512]{1,0:T(8,128)(2,1)} %q_ref.1, bf16[1024,512]{1,0:T(8,128)(2,1)} %k_ref.1, bf16[1024,512]{1,0:T(8,128)(2,1)} %v_ref.1, f32[1,1024]{1,0:T(1,128)} %rate_ref.1, s32[1,2]{1,0:T(1,128)} %win_ref.1, bf16[1,512,512]{2,1,0:T(8,128)(2,1)} %w1_ref.1, bf16[1,512,512]{2,1,0:T(8,128)(2,1)} %w3_ref.1, ...), custom_call_target="tpu_custom_call" | custom-call | flops 13400000512 | bytes 15000000 | tf_op jit(solution)/shard_map/ttt_layer/pallas_call | solution.py:558
  104.7 2.5 %copy.12 = bf16[1024,640]{1,0:T(8,128)(2,1)} copy(bf16[1024,640]{1,0:T(8,128)(2,1)} %ttt_layer.1) | data formatting | bytes 2621440

commit v4 on v3

--- a/solution.py
+++ b/solution.py
@@ -27,7 +27,10 @@
 NG = MY // GT
 PT = 128
 NP = MY // PT
+OUT_PARTS = ((0, 128), (128, 128), (256, 128), (384, 64), (448, 64))
 WP = HEADS // 2
+ONE_LAG = 0
+TWO_LAG = 2
 HP = 128
 GRAD_LIMIT = 24.0
 EPS = 1e-6
@@ -60,7 +63,7 @@
     q, k, v, hk, hv, stage, w1, w3, w2, wo, rate, gain,
     hid, tgt, bg, bu,
     sib_send, sib_recv, own, rs_send, rs_recv, x_send, x_recv, gfull,
-    n1, n3, n2, m_run, l_run, acc, gat, oth, wo2, sum_here, sum_pair, opair, outv,
+    n1, n3, n2, m_run, l_run, acc, gat, oth, wo2, opair, outv,
     load_sem, out_sem, halo_ss, halo_rs, stage_ss, stage_rs, sib_ss, sib_rs, rs_ss, rs_rs, x_ss, x_rs,
     ag_ss, ag_rs, sg_ss, sg_rs, g_ss, g_rs, w_ss, w_rs, ws_ss, ws_rs, o_ss, o_rs,
 ):
@@ -101,12 +104,14 @@
         pl.semaphore_signal(bar, inc=1, device_id=p, device_id_type=MESH)
 
     loads = []
+    lo, hi = pl.ds(0, TOK // 2), pl.ds(TOK // 2, TOK // 2)
     for i, (src, dst) in enumerate(
-        ((k_ref, k), (w1_ref, w1), (w3_ref, w3), (w2_ref, w2), (rate_ref, rate), (v_ref, v),
+        ((k_ref.at[lo], k.at[lo]), (w1_ref, w1), (w3_ref, w3), (rate_ref, rate),
+         (v_ref.at[lo], v.at[lo]), (w2_ref, w2), (k_ref.at[hi], k.at[hi]), (v_ref.at[hi], v.at[hi]),
          (q_ref, q), (gain_ref, gain), (wo_ref, wo))
     ):
         c = pltpu.make_async_copy(src, dst, load_sem.at[i])
-        if i < 6:
+        if i < 8:
             c.start()
         loads.append(c)
 
@@ -179,8 +184,6 @@
 
     for c in loads[:6]:
         c.wait()
-    for c in loads[6:]:
-        c.start()
 
     def grad_tile(t, carry):
         r = pl.ds(pl.multiple_of(t * TT, TT), TT)
@@ -206,21 +209,39 @@
     pl.semaphore_wait(bar, len(partners))
     push(6)
 
-    def w_rows(cc, i):
-        return pl.ds(pl.multiple_of((cc * WP + i) * HD, HD), HD)
-
-    for i in range(WP):
-        r = w_rows(core, i)
-        send(wo_ref.at[r], wo2.at[r], w_ss.at[i], w_rs.at[i], pair)
-
+    keep = 2 + z % 2
+    lack = 3 - z % 2
+    half_rows = HD // 2
+
+    def w_at(cc, i, lo=0, n=HD):
+        return wo2.at[pl.ds(pl.multiple_of((cc * WP + i) * HD + lo, half_rows), n)]
+
+    def w_part(cc, j):
+        return (
+            w_at(cc, keep), w_at(cc, 0), w_at(cc, 1),
+            w_at(cc, lack, 0, half_rows), w_at(cc, lack, half_rows, half_rows),
+        )[j]
+
+    for j, i in enumerate((keep, 0, 1)):
+        r = pl.ds(pl.multiple_of((core * WP + i) * HD, HD), HD)
+        send(wo_ref.at[r], wo2.at[r], w_ss.at[j], w_rs.at[j], pair)
+
+    def w_swap():
+        for way in range(2):
+            r = w_at(core, keep, way * half_rows, half_rows)
+            send(r, r, w_ss.at[3 + way], w_rs.at[3 + way], zway[way])
+
+    for c in loads[6:8]:
+        c.wait()
+    for c in loads[8:]:
+        c.start()
     lax.fori_loop(2, NT, grad_tile, 0)
     push(3)
 
-    def w_on(i):
-        r = wo2.at[w_rows(core, i)]
-        arrived(r, w_rs.at[i])
-        send(r, r, ws_ss.at[i], ws_rs.at[i], sib)
-
+    def w_on(j):
+        r = w_part(core, j)
+        arrived(r, w_rs.at[j])
+        send(r, r, ws_ss.at[j], ws_rs.at[j], sib)
 
     theirs = pl.ds(pl.multiple_of((1 - core) * HALF, HALF), HALF)
     mine = pl.ds(pl.multiple_of(core * HALF, HALF), HALF)
@@ -228,14 +249,8 @@
     for m, (a, b) in enumerate(pairs):
         sib_send[m] = dot_tn(a[:, theirs], b[...]).astype(BF16)
         send(sib_send.at[m], sib_recv.at[m], sib_ss.at[m], sib_rs.at[m], sib)
-    for m, (a, b) in enumerate(pairs):
-        own[m] = dot_tn(a[:, mine], b[...])
-
-    for m in range(3):
-        arrived(sib_recv.at[m], sib_rs.at[m])
-        own[m] = own[m] + sib_recv[m].astype(F32)
-
-    for c in loads[6:8]:
+
+    for c in loads[8:10]:
         c.wait()
     scale = HD ** -0.5
     reach = [win_ref[0, 0], win_ref[0, 1]]
@@ -290,6 +305,11 @@
 
     for step in range(1, HOPS + 1):
         for m in range(3):
+            if step == 1:
+                a, b = pairs[m]
+                own[m] = dot_tn(a[:, mine], b[...])
+                arrived(sib_recv.at[m], sib_rs.at[m])
+                own[m] = own[m] + sib_recv[m].astype(F32)
             for way in range(2):
                 if not goes(m, way, step):
                     continue
@@ -304,7 +324,8 @@
                     rs_ss.at[m, way, step - 1], rs_rs.at[m, way, step - 1], zway[way],
                 )
         push(1)
-        pass_values(2 if step == 1 else 1)
+        if step > 1:
+            pass_values(1)
         own_tile(step - 1)
 
     for m in range(3):
@@ -315,7 +336,7 @@
         x_send[m] = part.astype(BF16)
         send(x_send.at[m], x_recv.at[m], x_ss.at[m], x_rs.at[m], xhp)
     push(2)
-    pass_values(1)
+    pass_values(2)
 
     def rows_of(d, cc):
         return pl.ds(pl.multiple_of(cc * HALF + ((z + NZ + d) % NZ) * SHARD, SHARD), SHARD)
@@ -347,14 +368,21 @@
                 if dist + 1 < HOPS or (dist + 1 == HOPS and far_way(m) == way):
                     to_ring(m, d, way, dist + 1)
                 to_core(m, d)
-        if dist < 3:
-            push(2 - dist)
+        if dist == 1:
+            push(1)
+        if dist < HOPS:
             pass_values(1)
-
-    w_on(0)
+        if dist == 1:
+            w_on(0)
+        if dist == HOPS - 1:
+            w_swap()
+            pulled(0, 8)
+            halo_tile(2)
+            halo_tile(3)
+
     w_on(1)
-    pulled(0, len(pieces))
-    for t in range(NT):
+    pulled(8, len(pieces))
+    for t in range(NT // 2):
         halo_tile(t)
 
     squares = jnp.zeros((1, HD), F32)
@@ -438,22 +466,28 @@
         got(x_pair if t % 2 == 0 else h_far, t)
         got(x_far, t)
 
-    def heads_dot(heads, r, w):
-        o = None
-        for h in heads:
-            p = dot(gat[h, r, :], w[pl.ds(pl.multiple_of(h * HD, HD), HD), :])
-            o = p if o is None else o + p
-        return o
-
-    near = (h_own, h_mate, x_own, x_mate)
-    distant = (h_pair, h_far, x_pair, x_far)
+    def place(i):
+        return pl.ds(i * PT, PT), pl.ds(pl.multiple_of(group * MY + i * PT, PT), PT)
+
+    def all_heads(r, w):
+        o = dot(gat[0, r, :], w[pl.ds(0, HD), :])
+        for h in range(1, HEADS):
+            o = o + dot(gat[h, r, :], w[pl.ds(h * HD, HD), :])
+        return o.astype(BF16)
+
+    def out_part(half, j):
+        lo, n = OUT_PARTS[j]
+        return pl.ds(pl.multiple_of(half * MY + lo, GT), n)
+
+    def project_pair(j):
+        lo, n = OUT_PARTS[j]
+        r = pl.ds(lo, n)
+        opair[r, :] = all_heads(r, wo2)
+        send(opair.at[r], outv.at[out_part(group, j)], o_ss.at[j], o_rs.at[j], pair)
 
     def project(i):
-        r = pl.ds(i * PT, PT)
-        here = pl.ds(pl.multiple_of(group * MY + i * PT, PT), PT)
-        opair[r, :] = (sum_pair[r, :] + heads_dot(distant, r, wo2)).astype(BF16)
-        send(opair.at[r], outv.at[here], o_ss.at[i], o_rs.at[i], pair)
-        outv[here, :] = (sum_here[r, :] + heads_dot(distant, r, wo)).astype(BF16)
+        r, here = place(i)
+        outv[here, :] = all_heads(r, wo)
         pltpu.make_async_copy(outv.at[here], out_ref.at[here], out_sem.at[0, i]).start()
 
     for i in range(MY // TT):
@@ -464,63 +498,50 @@
         oth[r, :] = readout(1 - group, i)
         for t in range(i * TT // GT, (i + 1) * TT // GT):
             other_out(t)
-    w_on(2)
-    loads[8].wait()
-
-    def sum_up(i):
-        r = pl.ds(i * TT, TT)
-        sum_here[r, :] = heads_dot(near, r, wo)
-
-    def sum_up_pair(i):
-        r = pl.ds(i * TT, TT)
-        sum_pair[r, :] = heads_dot(near, r, wo2)
-
-    for t in range(NG):
-        near_one(t)
-    w_on(3)
-    for t in (0, 1):
-        pair_one(t)
-    for t in range(4):
-        near_rest(t)
-    sum_up(0)
-    for t in (2, 3):
-        pair_one(t)
-    for t in (0, 1):
-        pair_two(t)
-    for t in range(4, 8):
-        near_rest(t)
-    sum_up(1)
-    for t in (4, 5):
-        pair_one(t)
-    for t in (2, 3):
-        pair_two(t)
-    for i in range(WP):
-        arrived(wo2.at[w_rows(1 - core, i)], ws_rs.at[i])
-    sum_up_pair(0)
-    for t in (6, 7):
-        pair_one(t)
-    for t in (4, 5):
-        pair_two(t)
-    sum_up_pair(1)
-    for t in (0, 1):
-        pair_rest(t)
-    project(0)
-    for t in (6, 7):
-        pair_two(t)
-    for i in range(1, NP):
-        for t in (2 * i, 2 * i + 1):
-            pair_rest(t)
-        project(i)
-
+    loads[10].wait()
+    PER = PT // GT
+    for step in range(NG + 5):
+        if step < NG:
+            near_one(step)
+        if 0 <= step - ONE_LAG < NG:
+            pair_one(step - ONE_LAG)
+        if step == 1:
+            w_on(2)
+        if step == 2:
+            w_on(3)
+            w_on(4)
+        if 0 <= step - TWO_LAG < NG:
+            pair_two(step - TWO_LAG)
+        p = step - 4
+        if 0 <= p < NG:
+            near_rest(p)
+            pair_rest(p)
+            if p == PER - 1:
+                for j in range(WP + 1):
+                    arrived(w_part(1 - core, j), ws_rs.at[j])
+            if (p + 1) % PER == 0:
+                i = p // PER
+                if i < NP - 1:
+                    project_pair(i)
+                if i < NP - 2:
+                    project(i)
+            if p == NG - 2:
+                project_pair(NP - 1)
+            if p == NG - 1:
+                project_pair(NP)
+    project(NP - 2)
+    project(NP - 1)
+
+    for j in range(NP + 1):
+        there = out_part(1 - group, j)
+        arrived(outv.at[there], o_rs.at[j])
+        pltpu.make_async_copy(outv.at[there], out_ref.at[there], out_sem.at[1, j]).start()
     for i in range(NP):
-        there = pl.ds(pl.multiple_of((1 - group) * MY + i * PT, PT), PT)
-        arrived(outv.at[there], o_rs.at[i])
-        pltpu.make_async_copy(outv.at[there], out_ref.at[there], out_sem.at[1, i]).start()
-    for i in range(NP):
-        for j in range(2):
-            half = group if j == 0 else 1 - group
-            r = pl.ds(pl.multiple_of(half * MY + i * PT, PT), PT)
-            pltpu.make_async_copy(outv.at[r], out_ref.at[r], out_sem.at[j, i]).wait()
+        r = place(i)[1]
+        pltpu.make_async_copy(outv.at[r], out_ref.at[r], out_sem.at[0, i]).wait()
+    for j in range(NP + 1):
+        r = out_part(1 - group, j)
+        pltpu.make_async_copy(outv.at[r], out_ref.at[r], out_sem.at[1, j]).wait()
     for c in sends:
         c.wait_send()
 
@@ -528,6 +549,10 @@
     def _():
         for c in passed:
             c.wait_send()
+
+
+def hand_over(src, dst):
+    dst[...] = src[...]
 
 
 def per_device(*args):
@@ -548,14 +573,14 @@
         V((HD, HD), BF16), V((HD, HD), BF16), V((HD, HD), BF16),
         V((TOK, 1), F32), V((TOK, 1), F32), V((TOK, HD), F32),
         V((HEADS, MY, HD), BF16), V((MY, HD), BF16),
-        V((HEADS * HD, COLS), BF16), V((MY, COLS), F32), V((MY, COLS), F32),
+        V((HEADS * HD, COLS), BF16),
         V((MY, COLS), BF16), V((TOK, COLS), BF16),
-        D((9,)), D((2, NP)), D((16,)), D((16,)), D((16,)), D((16,)), D((3,)), D((3,)),
+        D((11,)), D((2, NP + 1)), D((16,)), D((16,)), D((16,)), D((16,)), D((3,)), D((3,)),
         D((3, 2, HOPS)), D((3, 2, HOPS)), D((3,)), D((3,)),
         D((3, 2, HOPS)), D((3, 2, HOPS)), D((3, NZ)), D((3, NZ)),
-        D((NG, 7)), D((NG, HEADS)), D((WP,)), D((WP,)), D((WP,)), D((WP,)), D((NP,)), D((NP,)),
+        D((NG, 7)), D((NG, HEADS)), D((WP + 1,)), D((WP + 1,)), D((WP + 1,)), D((WP + 1,)), D((NP + 1,)), D((NP + 1,)),
     ]
-    return pl.pallas_call(
+    out = pl.pallas_call(
         body,
         out_shape=jax.ShapeDtypeStruct((TOK, COLS), BF16),
         in_specs=in_specs,
@@ -567,6 +592,15 @@
         cost_estimate=pl.CostEstimate(flops=13_400_000_000, bytes_accessed=15_000_000, transcendentals=3_000_000),
         name="ttt_layer",
     )(*args)
+    return pl.pallas_call(
+        hand_over,
+        out_shape=jax.ShapeDtypeStruct((TOK, COLS), BF16),
+        grid=(2,),
+        in_specs=[pl.BlockSpec((TOK // 2, COLS), lambda i: (i, 0))],
+        out_specs=pl.BlockSpec((TOK // 2, COLS), lambda i: (i, 0)),
+        cost_estimate=pl.CostEstimate(flops=0, bytes_accessed=4 * TOK * COLS, transcendentals=0),
+        name="hand_over",
+    )(out)
 
 
 def solution(mesh):

time: 107 us -> 102 us (0.953)
  Pallas kernels: 105 us -> 102 us
  local copies, waits for them, and re-layouts: 2.49 us -> 0 us
    pallas_call x1, Pallas kernels: 105 us -> 99.7 us  [per_device(): pl.pallas_call(body, out_shape=jax.ShapeDtypeStruct((TOK, COLS), BF16), i...]
    unnamed x1 -> x0, local copies, waits for them, and re-layouts: 2.49 us -> none
    pallas_call x0 -> x1, Pallas kernels: none -> 2.2 us  [per_device(): pl.pallas_call(hand_over, out_shape=jax.ShapeDtypeStruct((TOK, COLS), BF1...]
where the time goes in v4:
time: 102 us
  Pallas kernels  102 us (100%)
    pallas_call x1, Pallas kernels, per_device(): pl.pallas_call(body, out_shape=jax.ShapeDtypeStruct((TOK, COLS), BF16), i...  99.7 us
    pallas_call x1, Pallas kernels, per_device(): pl.pallas_call(hand_over, out_shape=jax.ShapeDtypeStruct((TOK, COLS), BF1...  2.2 us

profile of v4, /device:TPU:2, one launch (start us, length us, event | category | flops | bytes accessed | tf_op | source)
XLA Modules:
  0.0 101.9 jit_solution(15870600835238027675)
XLA Ops:
  0.0 99.7 %ttt_layer.1.src = bf16[1024,640]{1,0:T(8,128)(2,1)} custom-call(bf16[1024,512]{1,0:T(8,128)(2,1)} %q_ref.1, bf16[1024,512]{1,0:T(8,128)(2,1)} %k_ref.1, bf16[1024,512]{1,0:T(8,128)(2,1)} %v_ref.1, f32[1,1024]{1,0:T(1,128)} %rate_ref.1, s32[1,2]{1,0:T(1,128)} %win_ref.1, bf16[1,512,512]{2,1,0:T(8,128)(2,1)} %w1_ref.1, bf16[1,512,512]{2,1,0:T(8,128)(2,1)} %w3_ref.1, ...), custom_call_target="tpu_custom_call" | custom-call | flops 13400000512 | bytes 15000000 | tf_op jit(solution)/shard_map/ttt_layer/pallas_call | solution.py:583
  99.7 2.2 %hand_over.1 = bf16[1024,640]{1,0:T(8,128)(2,1)} custom-call(bf16[1024,640]{1,0:T(8,128)(2,1)} %ttt_layer.1.src), custom_call_target="tpu_custom_call" | custom-call | bytes 2621440 | tf_op jit(solution)/shard_map/hand_over/pallas_call | solution.py:595

commit v5 on v4

--- a/solution.py
+++ b/solution.py
@@ -30,7 +30,8 @@
 OUT_PARTS = ((0, 128), (128, 128), (256, 128), (384, 64), (448, 64))
 WP = HEADS // 2
 ONE_LAG = 0
-TWO_LAG = 2
+TWO_LAG = 3
+REST_LAG = 6
 HP = 128
 GRAD_LIMIT = 24.0
 EPS = 1e-6
@@ -500,7 +501,7 @@
             other_out(t)
     loads[10].wait()
     PER = PT // GT
-    for step in range(NG + 5):
+    for step in range(NG + REST_LAG):
         if step < NG:
             near_one(step)
         if 0 <= step - ONE_LAG < NG:
@@ -512,7 +513,7 @@
             w_on(4)
         if 0 <= step - TWO_LAG < NG:
             pair_two(step - TWO_LAG)
-        p = step - 4
+        p = step - REST_LAG
         if 0 <= p < NG:
             near_rest(p)
             pair_rest(p)
@@ -595,9 +596,9 @@
     return pl.pallas_call(
         hand_over,
         out_shape=jax.ShapeDtypeStruct((TOK, COLS), BF16),
-        grid=(2,),
-        in_specs=[pl.BlockSpec((TOK // 2, COLS), lambda i: (i, 0))],
-        out_specs=pl.BlockSpec((TOK // 2, COLS), lambda i: (i, 0)),
+        grid=(4,),
+        in_specs=[pl.BlockSpec((TT, COLS), lambda i: (i, 0))],
+        out_specs=pl.BlockSpec((TT, COLS), lambda i: (i, 0)),
         cost_estimate=pl.CostEstimate(flops=0, bytes_accessed=4 * TOK * COLS, transcendentals=0),
         name="hand_over",
     )(out)

time: 102 us -> 104 us (1.020)
    pallas_call x1, Pallas kernels: 2.2 us -> 3.48 us  [per_device(): pl.pallas_call(hand_over, out_shape=jax.ShapeDtypeStruct((TOK, COLS), BF1...]
where the time goes in v5:
time: 104 us; the launch traced here: 103 us
  Pallas kernels  103 us (99%)
    pallas_call x1, Pallas kernels, per_device(): pl.pallas_call(body, out_shape=jax.ShapeDtypeStruct((TOK, COLS), BF16), i...  99.6 us
    pallas_call x1, Pallas kernels, per_device(): pl.pallas_call(hand_over, out_shape=jax.ShapeDtypeStruct((TOK, COLS), BF1...  3.48 us

profile of v5, /device:TPU:2, one launch (start us, length us, event | category | flops | bytes accessed | tf_op | source)
XLA Modules:
  0.0 103.0 jit_solution(13684679241170652135)
XLA Ops:
  0.0 99.6 %ttt_layer.1.src = bf16[1024,640]{1,0:T(8,128)(2,1)} custom-call(bf16[1024,512]{1,0:T(8,128)(2,1)} %q_ref.1, bf16[1024,512]{1,0:T(8,128)(2,1)} %k_ref.1, bf16[1024,512]{1,0:T(8,128)(2,1)} %v_ref.1, f32[1,1024]{1,0:T(1,128)} %rate_ref.1, s32[1,2]{1,0:T(1,128)} %win_ref.1, bf16[1,512,512]{2,1,0:T(8,128)(2,1)} %w1_ref.1, bf16[1,512,512]{2,1,0:T(8,128)(2,1)} %w3_ref.1, ...), custom_call_target="tpu_custom_call" | custom-call | flops 13400000512 | bytes 15000000 | tf_op jit(solution)/shard_map/ttt_layer/pallas_call | solution.py:584
  99.6 3.5 %hand_over.1 = bf16[1024,640]{1,0:T(8,128)(2,1)} custom-call(bf16[1024,640]{1,0:T(8,128)(2,1)} %ttt_layer.1.src), custom_call_target="tpu_custom_call" | custom-call | bytes 2621440 | tf_op jit(solution)/shard_map/hand_over/pallas_call | solution.py:596
